TPU v7x, 768 devices: a whole 4x8x12 slice. The times are simulated.
768 devices in a mesh: grp: 16 (over y, core), shard: 48 (over x, z).
Axes of the slice: x: 4, y: 8, z: 12, core: 2. Of those that a mesh axis runs over, the one named last changes fastest.
Arguments:
- events: bfloat16 [98304, 1024], P(('grp', 'shard')), may hold values from -6 to 6
- user_ids: int32 [98304], P(('grp', 'shard')), may hold values from 0 to 191, as said below
- session_break: int32 [98304], P(('grp', 'shard')), may hold values 0 or 1
- in_gain: float32 [1024], replicated, may hold values from 0.1 to 1.9
- in_weight: bfloat16 [1024, 2048], replicated, may hold values from -0.1875 to 0.1875
- decay_rates: float32 [1024], replicated, may hold values from 0.0001 to 0.04
- keep_factor: float32 [1024], replicated, may hold values from 0.4 to 0.8
- out_gain: float32 [1024], replicated, may hold values from 0.1 to 1.9
- out_weight: bfloat16 [1024, 1024], replicated, may hold values from -0.1875 to 0.1875
Outputs:
- mixed: bfloat16 [98304, 1024], P(('grp', 'shard'))
Inputs may be any that keep to these rules, and one draw needn't show every extreme that they name: The owner range of an event is user_ids // 4. In every aligned block of 128 rows at most 7 rows share an owner range; in every aligned stretch of 6144 rows one owner range has exactly 7 rows in each of its blocks.
All inputs are finite; a program needn't handle non-finite values. No bound on the sum of `session_break` on one device may be relied on, other than what follows from the above.
Results may differ from a plain program's by a relative error of at most 0.0057.
Values may be sent and summed in bfloat16 or wider, within the bound.
A program may use at most 64 MiB of HBM per device.

v0:
```python
import jax
import jax.numpy as jnp
from jax import lax
from jax.sharding import PartitionSpec as P

U_DEV = 4


def carried_in(shard, axis, combine, identity):
    length, index = (lax.axis_size(axis), lax.axis_index(axis))
    everything = jax.tree.map(lambda part: lax.all_gather(part, axis), shard)
    start = jax.tree.map(
        lambda part, zero: jnp.broadcast_to(jnp.asarray(zero, part.dtype), part.shape),
        shard,
        identity,
    )

    def lap(k, before):
        reached = k < index
        new = combine(before, jax.tree.map(lambda part: part[k], everything))
        return jax.tree.map(lambda a, b: jnp.where(reached, a, b), new, before)

    return lax.fori_loop(0, length, lap, start)


def rms_scale(values, gain_vec):
    return values * lax.rsqrt(jnp.mean(values * values, axis=-1, keepdims=True) + 1e-06) * gain_vec


def project(source_rows, in_gain, in_weight):
    normed = rms_scale(source_rows.astype(jnp.float32), in_gain).astype(jnp.bfloat16)
    return jnp.dot(normed, in_weight, preferred_element_type=jnp.float32).astype(jnp.bfloat16)


def combine(earlier_pair, later_pair):
    return (earlier_pair[0] * later_pair[0], later_pair[0] * earlier_pair[1] + later_pair[1])


def mask_product(mask_rows, data_rows):
    return jnp.dot(mask_rows, data_rows, preferred_element_type=jnp.float32)


def exact_einsum(form, left, right):
    return jnp.einsum(form, left, right.astype(jnp.float32), precision=lax.Precision.HIGHEST)


def on_device(
    events,
    user_ids,
    session_break,
    in_gain,
    in_weight,
    decay_rates,
    keep_factor,
    out_gain,
    out_weight,
):
    owners = lax.axis_size("shard")
    local_rows, feature_width = events.shape
    capacity = 2 * local_rows // owners + 2
    slot_count = owners * capacity
    destination = user_ids // U_DEV
    onehot_dest = (destination[:, None] == jnp.arange(owners, dtype=jnp.int32)[None, :]).astype(
        jnp.bfloat16
    )
    row_index = jnp.arange(local_rows, dtype=jnp.int32)
    earlier = (row_index[:, None] > row_index[None, :]).astype(jnp.bfloat16)
    slot_rank = jnp.sum(
        mask_product(earlier, onehot_dest) * onehot_dest.astype(jnp.float32), axis=1
    ).astype(jnp.int32)
    slot_index = destination * capacity + slot_rank
    send_users = jnp.full((slot_count,), -1, jnp.int32).at[slot_index].set(user_ids % U_DEV)
    send_breaks = jnp.zeros((slot_count,), jnp.int32).at[slot_index].set(session_break)
    send_rows = jnp.zeros((slot_count, feature_width), jnp.bfloat16).at[slot_index].set(events)
    got_rows, got_users, got_breaks = (
        lax.all_to_all(send_rows, "shard", split_axis=0, concat_axis=0, tiled=True),
        lax.all_to_all(send_users, "shard", split_axis=0, concat_axis=0, tiled=True),
        lax.all_to_all(send_breaks, "shard", split_axis=0, concat_axis=0, tiled=True),
    )
    projected = project(got_rows, in_gain, in_weight)
    gate_part = projected[:, :feature_width].astype(jnp.float32)
    value_part = projected[:, feature_width:].astype(jnp.float32)
    member = (got_users[:, None] == jnp.arange(U_DEV, dtype=jnp.int32)[None, :]).astype(jnp.float32)
    valid_rows = jnp.sum(member, axis=1)
    tally_cols = jnp.stack([valid_rows, got_breaks.astype(jnp.float32) * valid_rows], axis=1)
    member_blocks = member.reshape(owners, capacity, U_DEV)
    tally_blocks = tally_cols.reshape(owners, capacity, 2)
    value_blocks = value_part.reshape(owners, capacity, feature_width)
    slot_pos = jnp.arange(capacity, dtype=jnp.int32)
    causal = (slot_pos[:, None] >= slot_pos[None, :]).astype(jnp.float32)
    within = exact_einsum("kiu,kju->kij", member_blocks, member_blocks) * causal[None, :, :]
    counts_pair = exact_einsum("kij,kjt->kit", within, tally_blocks)
    log_keep = jnp.log(keep_factor)
    log_level = -decay_rates * counts_pair[:, :, 0:1] + log_keep * counts_pair[:, :, 1:2]
    growth = jnp.exp(log_level)
    scaled = jnp.exp(-log_level) * value_blocks
    local_state = growth * exact_einsum("kij,kjd->kid", within, scaled)
    totals = exact_einsum("kiu,kit->kut", member_blocks, tally_blocks)
    piece_span = jnp.exp(-decay_rates * totals[:, :, 0:1] + log_keep * totals[:, :, 1:2])
    piece_ends = piece_span * exact_einsum("kiu,kid->kud", member_blocks, scaled)
    inclusive = lax.associative_scan(combine, (piece_span, piece_ends), axis=0)
    prefix_span = jnp.concatenate([jnp.ones_like(piece_span[:1]), inclusive[0][:-1]], axis=0)
    prefix_ends = jnp.concatenate([jnp.zeros_like(piece_ends[:1]), inclusive[1][:-1]], axis=0)
    block_span = inclusive[0][-1]
    block_ends = inclusive[1][-1]
    identity = (jnp.ones_like(block_span), jnp.zeros_like(block_ends))
    carry_start = carried_in((block_span, block_ends), "grp", combine, identity)[1]
    piece_start = prefix_span * carry_start[None, :, :] + prefix_ends
    hidden_blocks = local_state + growth * exact_einsum("kiu,kud->kid", member_blocks, piece_start)
    hidden = hidden_blocks.reshape(slot_count, feature_width)
    mixed_part = (rms_scale(hidden, out_gain) * jax.nn.silu(gate_part)).astype(jnp.bfloat16)
    back_rows = (
        got_rows.astype(jnp.float32)
        + jnp.dot(mixed_part, out_weight, preferred_element_type=jnp.float32)
    ).astype(jnp.bfloat16)
    returned = lax.all_to_all(back_rows, "shard", split_axis=0, concat_axis=0, tiled=True)[
        slot_index
    ]
    return returned


def solution(mesh):
    return jax.shard_map(
        on_device,
        mesh=mesh,
        in_specs=(
            P(("grp", "shard"), None),
            P(("grp", "shard")),
            P(("grp", "shard")),
            P(),
            P(),
            P(),
            P(),
            P(),
            P(),
        ),
        out_specs=P(("grp", "shard"), None),
        check_vma=False,
    )
```

profile of v0, /device:TPU:6, one launch (start us, length us, event | category | flops | bytes accessed | tf_op | source)
XLA Modules:
  0.0 319.1 jit_solution(5389876884091033967)
XLA Ops:
  2.8 18.5 %all-to-all-start.2 = ((s32[48,7,1]{1,2,0:T(1,128)}), s32[48,7,1]{1,2,0:T(1,128)S(1)}, u32[]{:S(2)}, u32[]{:S(2)}) async-start(s32[48,7,1]{1,2,0:T(1,128)} %bitcast.2), calls=%async_computation.2 | async-start | bytes 49152 | tf_op jit(solution)/shard_map/all_to_all | solution.py:78
  23.1 8.6 %all-to-all-done.2 = s32[48,7,1]{1,2,0:T(1,128)S(1)} async-done(((s32[48,7,1]{1,2,0:T(1,128)}), s32[48,7,1]{1,2,0:T(1,128)S(1)}, u32[]{:S(2)}, u32[]{:S(2)}) %all-to-all-start.2) | async-done | bytes 1376 | tf_op jit(solution)/shard_map/all_to_all | solution.py:78
  31.7 6.4 %all-to-all-start.1 = ((s32[48,7,1]{1,2,0:T(1,128)}), s32[48,7,1]{1,2,0:T(1,128)S(1)}, u32[]{:S(2)}, u32[]{:S(2)}) async-start(s32[48,7,1]{1,2,0:T(1,128)} %bitcast), calls=%async_computation.1 | async-start | bytes 49152 | tf_op jit(solution)/shard_map/all_to_all | solution.py:77
  41.1 7.3 %all-to-all-done.1 = s32[48,7,1]{1,2,0:T(1,128)S(1)} async-done(((s32[48,7,1]{1,2,0:T(1,128)}), s32[48,7,1]{1,2,0:T(1,128)S(1)}, u32[]{:S(2)}, u32[]{:S(2)}) %all-to-all-start.1) | async-done | bytes 1376 | tf_op jit(solution)/shard_map/all_to_all | solution.py:77
  48.4 6.5 %all-to-all-start = ((bf16[48,7,1024]{2,1,0:T(8,128)(2,1)}), bf16[48,7,1024]{2,1,0:T(8,128)(2,1)S(1)}, u32[]{:S(2)}, u32[]{:S(2)}) async-start(bf16[48,7,1024]{2,1,0:T(8,128)(2,1)} %all_to_all.26), calls=%async_computation | async-start | bytes 1572864 | tf_op jit(solution)/shard_map/all_to_all | solution.py:76
  59.1 24.3 %all-to-all-done = bf16[48,7,1024]{2,1,0:T(8,128)(2,1)S(1)} async-done(((bf16[48,7,1024]{2,1,0:T(8,128)(2,1)}), bf16[48,7,1024]{2,1,0:T(8,128)(2,1)S(1)}, u32[]{:S(2)}, u32[]{:S(2)}) %all-to-all-start) | async-done | bytes 688160 | tf_op jit(solution)/shard_map/all_to_all | solution.py:76
  85.1 4.3 %convolution_convert_fusion = bf16[336,2048]{1,0:T(8,128)(2,1)S(1)} fusion(bf16[1024,2048]{1,0:T(8,128)(2,1)} %param.15, f32[336,1024]{1,0:T(8,128)} %reshape.93, f32[1024]{0:T(1024)S(1)} %copy-done.29, f32[336]{0:T(512)S(1)} %rsqrt.23), kind=kOutput, calls=%fused_computation.7 | convolution fusion | flops 1411006464 | bytes 6952256 | tf_op jit(solution)/shard_map/dot_general | solution.py:32
  92.0 3.1 convolution_multiply_fusion
  109.7 2.7 pad.66
  112.4 2.7 pad.77
  115.1 2.7 pad.76
  117.8 2.7 pad.67
  130.0 4.1 %pad.68 = f32[12,4,1024]{2,1,0:T(4,128)} pad(f32[6,4,1024]{2,1,0:T(4,128)} %pad_maximum_fusion.4, f32[]{:T(128)} %constant.71.clone.1), padding=0_1_1x0_0_0x0_0_0 | pad | bytes 294916 | tf_op jit(solution)/shard_map/pad | solution.py:101
  134.1 4.1 %pad.69 = f32[12,4,1024]{2,1,0:T(4,128)} pad(f32[6,4,1024]{2,1,0:T(4,128)} %add.193, f32[]{:T(128)} %constant.71.clone.1), padding=1_0_1x0_0_0x0_0_0 | pad | bytes 294916 | tf_op jit(solution)/shard_map/pad | solution.py:101
  138.2 4.1 %pad.79 = f32[12,4,1024]{2,1,0:T(4,128)} pad(f32[6,4,1024]{2,1,0:T(4,128)} %add.205, f32[]{:T(128)} %constant.71.clone.1), padding=1_0_1x0_0_0x0_0_0 | pad | bytes 294916 | tf_op jit(solution)/shard_map/pad | solution.py:101
  146.2 4.5 %pad.80 = f32[24,4,1024]{2,1,0:T(4,128)} pad(f32[12,4,1024]{2,1,0:T(4,128)S(1)} %pad_maximum_fusion.3, f32[]{:T(128)} %constant.71.clone.1), padding=0_1_1x0_0_0x0_0_0 | pad | bytes 589828 | tf_op jit(solution)/shard_map/pad | solution.py:101
  151.6 4.4 %pad.70 = f32[24,4,1024]{2,1,0:T(4,128)} pad(f32[12,4,1024]{2,1,0:T(4,128)S(1)} %pad_maximum_fusion.2, f32[]{:T(128)} %constant.71.clone.1), padding=0_1_1x0_0_0x0_0_0 | pad | bytes 589828 | tf_op jit(solution)/shard_map/pad | solution.py:101
  156.0 4.5 %pad.71 = f32[24,4,1024]{2,1,0:T(4,128)} pad(f32[12,4,1024]{2,1,0:T(4,128)S(1)} %add.194, f32[]{:T(128)} %constant.71.clone.1), padding=1_0_1x0_0_0x0_0_0 | pad | bytes 589828 | tf_op jit(solution)/shard_map/pad | solution.py:101
  160.5 4.4 %pad.81 = f32[24,4,1024]{2,1,0:T(4,128)} pad(f32[12,4,1024]{2,1,0:T(4,128)S(1)} %copy-done.14, f32[]{:T(128)} %constant.71.clone.1), padding=1_0_1x0_0_0x0_0_0 | pad | bytes 589828 | tf_op jit(solution)/shard_map/pad | solution.py:101
  166.2 2.8 add_multiply_fusion.2
  170.0 8.3 %pad.109 = f32[47,4,1024]{2,1,0:T(4,128)} pad(f32[24,4,1024]{2,1,0:T(4,128)S(1)} %pad_maximum_fusion.1, f32[]{:T(128)} %constant.71.clone.1), padding=0_0_1x0_0_0x0_0_0 | pad | bytes 1163268 | tf_op jit(solution)/shard_map/slice | solution.py:103
  178.3 8.3 %pad.82 = f32[48,4,1024]{2,1,0:T(4,128)} pad(f32[24,4,1024]{2,1,0:T(4,128)S(1)} %pad_maximum_fusion.1, f32[]{:T(128)} %constant.71.clone.1), padding=0_1_1x0_0_0x0_0_0 | pad | bytes 1179652 | tf_op jit(solution)/shard_map/pad | solution.py:101
  186.7 8.3 %pad.150 = f32[47,4,1024]{2,1,0:T(4,128)} pad(f32[24,4,1024]{2,1,0:T(4,128)S(1)} %add.195, f32[]{:T(128)} %constant.71.clone.1), padding=0_0_1x0_0_0x0_0_0 | pad | bytes 1163268
  194.9 8.3 %pad.73 = f32[48,4,1024]{2,1,0:T(4,128)} pad(f32[24,4,1024]{2,1,0:T(4,128)S(1)} %add.195, f32[]{:T(128)} %constant.71.clone.1), padding=1_0_1x0_0_0x0_0_0 | pad | bytes 1179652 | tf_op jit(solution)/shard_map/pad | solution.py:101
  203.2 8.9 %pad.148 = f32[48,4,1024]{2,1,0:T(4,128)S(1)} pad(f32[24,4,1024]{2,1,0:T(4,128)} %add.209, f32[]{:T(128)} %constant.71.clone.1), padding=1_0_1x0_0_0x0_0_0 | pad | bytes 1179652
  213.2 8.3 %pad.72 = f32[48,4,1024]{2,1,0:T(4,128)} pad(f32[24,4,1024]{2,1,0:T(4,128)S(1)} %pad_maximum_fusion, f32[]{:T(128)} %constant.71.clone.1), padding=0_1_1x0_0_0x0_0_0 | pad | bytes 1179652 | tf_op jit(solution)/shard_map/pad | solution.py:101
  224.5 18.3 %all_gather.7 = f32[16,4,1024]{2,1,0:T(4,128)S(1)} all-gather(f32[1,4,1024]{2,1,0:T(4,128)S(1)} %slice_add_fusion.5), channel_id=1, replica_groups=mesh['grp'=16,'shard'=48] {'grp'}, dimensions={0}, use_global_device_ids=true | all-gather | bytes 278528 | tf_op jit(solution)/shard_map/all_gather | solution.py:11
  242.8 16.0 %all_gather.6 = f32[16,4,1024]{2,1,0:T(4,128)S(1)} all-gather(f32[1,4,1024]{2,1,0:T(4,128)S(1)} %slice-done.2), channel_id=1, replica_groups=mesh['grp'=16,'shard'=48] {'grp'}, dimensions={0}, use_global_device_ids=true | all-gather | bytes 278528 | tf_op jit(solution)/shard_map/all_gather | solution.py:11
  262.6 3.4 %multiply_reduce_fusion = (f32[48,7]{1,0:T(8,128)S(1)}, f32[48,7,1024]{2,1,0:T(8,128)}) fusion(f32[48,7]{1,0:T(8,128)S(1)} %bitcast.40, f32[1024]{0:T(1024)S(1)} %log.3, f32[48,7]{1,0:T(8,128)S(1)} %bitcast.38, f32[1024]{0:T(1024)S(1)} %neg.11, f32[48,7,1024]{2,1,0:T(8,128)S(1)} %fusion.8, f32[48,7,7]{2,1,0:T(8,128)S(1)} %copy-done.13, ...), kind=kOutput, calls=%fused_computation.11 | convolution fusion | flops 33029808 | bytes 4150400 | tf_op jit(solution)/shard_map/kij,kjd->kid/dot_general | solution.py:44
  267.7 3.5 %fusion.6 = bf16[336,1024]{1,0:T(8,128)(2,1)} fusion(f32[336,1024]{1,0:T(8,128)} %reshape.93, bf16[1024,1024]{1,0:T(8,128)(2,1)S(1)} %copy-done, f32[336,1024]{1,0:T(8,128)S(1)} %reshape.92, bf16[336,2048]{1,0:T(8,128)(2,1)} %copy-done.17, f32[1024]{0:T(1024)S(1)} %copy-done.30, f32[336]{0:T(512)S(1)} %rsqrt.25), kind=kOutput, calls=%fused_computation.22 | convolution fusion | flops 708427776 | bytes 6231360 | tf_op jit(solution)/shard_map/dot_general | solution.py:114
  273.3 9.2 %all-to-all-start.3 = ((bf16[48,7,1024]{2,1,0:T(8,128)(2,1)}), bf16[48,7,1024]{2,1,0:T(8,128)(2,1)}, u32[]{:S(2)}, u32[]{:S(2)}) async-start(bf16[48,7,1024]{2,1,0:T(8,128)(2,1)} %all_to_all.32), calls=%async_computation.3 | async-start | bytes 1572864 | tf_op jit(solution)/shard_map/all_to_all | solution.py:116
  282.5 33.7 %all-to-all-done.3 = bf16[48,7,1024]{2,1,0:T(8,128)(2,1)} async-done(((bf16[48,7,1024]{2,1,0:T(8,128)(2,1)}), bf16[48,7,1024]{2,1,0:T(8,128)(2,1)}, u32[]{:S(2)}, u32[]{:S(2)}) %all-to-all-start.3) | async-done | bytes 688160 | tf_op jit(solution)/shard_map/all_to_all | solution.py:116
  (164 shorter events, 61.9 us)
Async XLA Ops:
  0.0 267.7 %copy-start = (bf16[1024,1024]{1,0:T(8,128)(2,1)S(1)}, bf16[1024,1024]{1,0:T(8,128)(2,1)}, u32[]{:S(2)}) copy-start(bf16[1024,1024]{1,0:T(8,128)(2,1)} %param.19) | copy-start | bytes 6291460
  1.0 47.4 %copy-start.27 = (s32[128]{0:T(128)}, s32[128]{0:T(128)S(1)}, u32[]{:S(2)}) copy-start(s32[128]{0:T(128)S(1)} %compare_select_fusion) | copy-start | bytes 1540
  2.8 28.9 %all-to-all-start.2 = ((s32[48,7,1]{1,2,0:T(1,128)}), s32[48,7,1]{1,2,0:T(1,128)S(1)}, u32[]{:S(2)}, u32[]{:S(2)}) async-start(s32[48,7,1]{1,2,0:T(1,128)} %bitcast.2), calls=%async_computation.2 | async-start | bytes 49152 | tf_op jit(solution)/shard_map/all_to_all | solution.py:78
  31.7 16.7 %all-to-all-start.1 = ((s32[48,7,1]{1,2,0:T(1,128)}), s32[48,7,1]{1,2,0:T(1,128)S(1)}, u32[]{:S(2)}, u32[]{:S(2)}) async-start(s32[48,7,1]{1,2,0:T(1,128)} %bitcast), calls=%async_computation.1 | async-start | bytes 49152 | tf_op jit(solution)/shard_map/all_to_all | solution.py:77
  40.0 15.0 %copy-start.25 = (f32[1024]{0:T(1024)S(1)}, f32[1024]{0:T(1024)}, u32[]{:S(2)}) copy-start(f32[1024]{0:T(1024)} %param.16) | copy-start | bytes 12292
  40.0 15.0 %copy-start.26 = (f32[1024]{0:T(1024)S(1)}, f32[1024]{0:T(1024)}, u32[]{:S(2)}) copy-start(f32[1024]{0:T(1024)} %param.17) | copy-start | bytes 12292
  48.4 35.0 %all-to-all-start = ((bf16[48,7,1024]{2,1,0:T(8,128)(2,1)}), bf16[48,7,1024]{2,1,0:T(8,128)(2,1)S(1)}, u32[]{:S(2)}, u32[]{:S(2)}) async-start(bf16[48,7,1024]{2,1,0:T(8,128)(2,1)} %all_to_all.26), calls=%async_computation | async-start | bytes 1572864 | tf_op jit(solution)/shard_map/all_to_all | solution.py:76
  57.2 27.9 %copy-start.18 = (f32[48,4,1]{1,2,0:T(1,128)}, f32[48,4,1]{1,2,0:T(1,128)S(1)}, u32[]{:S(2)}) copy-start(f32[48,4,1]{1,2,0:T(1,128)S(1)} %get-tuple-element.153) | copy-start | bytes 2308
  58.5 26.6 %copy-start.29 = (f32[1024]{0:T(1024)S(1)}, f32[1024]{0:T(1024)}, u32[]{:S(2)}) copy-start(f32[1024]{0:T(1024)} %param.14) | copy-start | bytes 12292
  92.0 3.1 copy-start.2
  95.0 1.7 copy-start.7
  98.1 1.3 copy-start.16
  108.3 17.2 %copy-start.22 = (f32[1,4,1024]{2,1,0:T(4,128)S(1)}, f32[1,4,1024]{2,1,0:T(4,128)}, u32[]{:S(2)}) copy-start(f32[1,4,1024]{2,1,0:T(4,128)} %slice.258) | copy-start | bytes 49156
  108.3 20.1 %copy-start.21 = (f32[1,4,1024]{2,1,0:T(4,128)S(1)}, f32[1,4,1024]{2,1,0:T(4,128)}, u32[]{:S(2)}) copy-start(f32[1,4,1024]{2,1,0:T(4,128)} %slice.241) | copy-start | bytes 49156
  134.1 12.0 %copy-start.20 = (f32[1,4,1024]{2,1,0:T(4,128)S(1)}, f32[1,4,1024]{2,1,0:T(4,128)}, u32[]{:S(2)}) copy-start(f32[1,4,1024]{2,1,0:T(4,128)} %slice.257) | copy-start | bytes 49156
  142.3 3.8 %copy-start.8 = (f32[12,4,1024]{2,1,0:T(4,128)S(1)}, f32[12,4,1024]{2,1,0:T(4,128)}, u32[]{:S(2)}) copy-start(f32[12,4,1024]{2,1,0:T(4,128)} %pad.68) | copy-start | bytes 589828
  142.3 3.8 %copy-start.9 = (f32[12,4,1024]{2,1,0:T(4,128)S(1)}, f32[12,4,1024]{2,1,0:T(4,128)}, u32[]{:S(2)}) copy-start(f32[12,4,1024]{2,1,0:T(4,128)} %pad.69) | copy-start | bytes 589828
  144.0 6.7 %copy-start.19 = (f32[1,4,1024]{2,1,0:T(4,128)S(1)}, f32[1,4,1024]{2,1,0:T(4,128)}, u32[]{:S(2)}) copy-start(f32[1,4,1024]{2,1,0:T(4,128)} %slice.240) | copy-start | bytes 49156
  146.0 14.5 %copy-start.14 = (f32[12,4,1024]{2,1,0:T(4,128)S(1)}, f32[12,4,1024]{2,1,0:T(4,128)}, u32[]{:S(2)}) copy-start(f32[12,4,1024]{2,1,0:T(4,128)} %add.207) | copy-start | bytes 589828
  166.2 2.8 copy-start.3
  166.2 2.8 copy-start.4
  166.2 3.7 %slice-start.1 = ((f32[48,4,1024]{2,1,0:T(4,128)}), f32[1,4,1024]{2,1,0:T(4,128)S(1)}, s32[]{:S(2)}) async-start(f32[48,4,1024]{2,1,0:T(4,128)} %copy-done.7), calls=%async_computation.5 | async-start | bytes 32768 | tf_op jit(solution)/shard_map/slice | solution.py:101
  186.7 25.4 %slice-start = ((f32[48,4,1024]{2,1,0:T(4,128)}), f32[1,4,1024]{2,1,0:T(4,128)S(1)}, s32[]{:S(2)}) async-start(f32[48,4,1024]{2,1,0:T(4,128)} %copy-done.1), calls=%async_computation.4 | async-start | bytes 32768 | tf_op jit(solution)/shard_map/slice | solution.py:101
  221.5 21.3 %slice-start.2 = ((f32[47,4,1024]{2,1,0:T(4,128)}), f32[1,4,1024]{2,1,0:T(4,128)S(1)}, s32[]{:S(2)}) async-start(f32[47,4,1024]{2,1,0:T(4,128)} %pad.150), calls=%async_computation.6 | async-start | bytes 32768 | tf_op jit(solution)/shard_map/slice | solution.py:104
  242.8 18.4 %copy-start.5 = (f32[47,4,1024]{2,1,0:T(4,128)S(1)}, f32[47,4,1024]{2,1,0:T(4,128)}, u32[]{:S(2)}) copy-start(f32[47,4,1024]{2,1,0:T(4,128)} %slice_add_fusion.9) | copy-start | bytes 2310148
  261.2 1.4 copy-start.10
  261.2 1.4 copy-start.13
  261.2 1.4 copy-start.23
  261.2 1.4 copy-start.24
  266.0 1.7 copy-start.30
  271.2 11.3 %copy-start.28 = (s32[128]{0:T(128)S(1)}, s32[128]{0:T(128)}, u32[]{:S(2)}) copy-start(s32[128]{0:T(128)} %copy-done.27) | copy-start | bytes 1540
  273.3 42.9 %all-to-all-start.3 = ((bf16[48,7,1024]{2,1,0:T(8,128)(2,1)}), bf16[48,7,1024]{2,1,0:T(8,128)(2,1)}, u32[]{:S(2)}, u32[]{:S(2)}) async-start(bf16[48,7,1024]{2,1,0:T(8,128)(2,1)} %all_to_all.32), calls=%async_computation.3 | async-start | bytes 1572864 | tf_op jit(solution)/shard_map/all_to_all | solution.py:116
  (6 other events, 6.5 us)
where the time goes:
time: 323 us; the launch traced here: 319 us
  local copies, waits for them, and re-layouts  121 us (37%)
  waiting for transfers between devices  73.9 us (23%)
  starting transfers between devices  40.6 us (13%)
  blocking collectives  34.2 us (11%)
  other arithmetic  32.3 us (10%)
  matrix products  16.6 us (5%)
    pad x17, local copies, waits for them, and re-layouts, on_device(): inclusive = lax.associative_scan(combine, (piece_span, piece_ends), axis=0)  72 us
    all_gather x2, blocking collectives, carried_in(): everything = jax.tree.map(lambda part: lax.all_gather(part, axis), shard)  34.2 us
    all_to_all x1, waiting for transfers between devices, on_device(): lax.all_to_all(back_rows, 'shard', split_axis=0, concat_axis=0, tiled=True)  33.7 us
    all_to_all x1, waiting for transfers between devices, on_device(): lax.all_to_all(send_rows, 'shard', split_axis=0, concat_axis=0, tiled=True)  24.3 us
    unnamed x64, local copies, waits for them, and re-layouts  18.7 us
    all_to_all x1, starting transfers between devices, on_device(): lax.all_to_all(send_breaks, 'shard', split_axis=0, concat_axis=0, tiled=T...  18.5 us
    add x10, other arithmetic, on_device(): inclusive = lax.associative_scan(combine, (piece_span, piece_ends), axis=0)  13.3 us
    all_to_all x1, starting transfers between devices, on_device(): lax.all_to_all(back_rows, 'shard', split_axis=0, concat_axis=0, tiled=True)  9.17 us
  transfers between devices with their start and end apart: 4, of which 4 were waited for; matrix products, arithmetic and copies ran while one was open for 2% of the time, Pallas kernels for 0%

commit v1 on v0

v1 whole, which is shorter than its diff:
```python
import functools

import jax
import jax.numpy as jnp
from jax import lax
from jax.experimental import pallas as pl
from jax.experimental.pallas import tpu as pltpu
from jax.sharding import PartitionSpec as P

F32, BF16 = jnp.float32, jnp.bfloat16
MESH = pl.DeviceIdType.MESH
NZ = 12
NT = 8
LANES = 128
ROWS = 128
USERS = 192


def dot(a, b):
    return jnp.dot(a, b, preferred_element_type=F32)


def decay_of(counts, rate, log_keep):
    breaks = jnp.floor(counts * (1.0 / 16.0))
    return log_keep * breaks - rate * (counts - 16.0 * breaks)


def kernel(
    NC, NX, NY,
    ev_ref, ids_ref, brk_ref, in_gain_ref, rate_ref, keep_ref, out_gain_ref, w_in, w_out,
    out_ref,
    wv, wg, wo, vt, id_src, idb, vbuf, mt, mem, dcy, span, pre_q, pre_p,
    end_e, end_q, s1e, s1q, slab_e, slab_q, ye, yq, cst, cbuf, cacc,
    rsrc, rbuf, xloc, grow, sgate, acc, lk_ref,
    w_sem, id_send, id_recv, v_send, v_recv, q1_send, q1_recv, e1_send, e1_recv,
    yq_send, yq_recv, ye_send, ye_recv, c_send, c_recv, r_send, r_recv,
):
    NP = NC * NX
    UP = USERS // NP
    g, s = lax.axis_index("grp"), lax.axis_index("shard")
    y, c = lax.div(g, NC), lax.rem(g, NC)
    x, z = lax.div(s, NZ), lax.rem(s, NZ)
    line = c * NX + x
    zq, zr = lax.div(z, 3), lax.rem(z, 3)
    holder = zr < 2
    tile = zq + 4 * zr

    def at_z(zz):
        return (g, x * NZ + zz)

    def at_line(p):
        return (y * NC + p // NX, (p % NX) * NZ + z)

    def at_y(yy):
        return (yy * NC + c, s)

    def rcopy(src, dst, ss, rs, dev):
        return pltpu.make_async_remote_copy(
            src_ref=src, dst_ref=dst, send_sem=ss, recv_sem=rs, device_id=dev, device_id_type=MESH
        )

    half = NT * LANES // 2
    full = NT * LANES
    wcopies = [
        pltpu.make_async_copy(w_in.at[:, pl.ds(full, half)], wv.at[0], w_sem.at[0]),
        pltpu.make_async_copy(w_in.at[:, pl.ds(full + half, half)], wv.at[1], w_sem.at[1]),
        pltpu.make_async_copy(w_in.at[:, pl.ds(0, full)], wg, w_sem.at[2]),
        pltpu.make_async_copy(w_out, wo, w_sem.at[3]),
    ]
    for cp in wcopies:
        cp.start()

    barrier = pltpu.get_barrier_semaphore()
    for d in range(1, NZ):
        pl.semaphore_signal(barrier, inc=1, device_id=at_z(lax.rem(z + d, NZ)), device_id_type=MESH)

    @pl.when(holder)
    def _():
        for d in range(1, NP):
            p = lax.rem(line + d, NP)
            pl.semaphore_signal(barrier, inc=1, device_id=(y * NC + lax.div(p, NX), lax.rem(p, NX) * NZ + z), device_id_type=MESH)
        for d in range(1, NY):
            pl.semaphore_signal(barrier, inc=1, device_id=at_y(lax.rem(y + d, NY)), device_id_type=MESH)

    idr = ids_ref[...].astype(F32)
    brk = brk_ref[...].astype(F32)
    id_src[...] = jnp.concatenate([idr, brk, jnp.zeros((6, LANES), F32)], axis=0)
    lk_ref[...] = jnp.log(keep_ref[...])
    ev = ev_ref[...].astype(F32)
    mean = jnp.sum(ev * ev, axis=1, keepdims=True) * (1.0 / full)
    normed = (ev * lax.rsqrt(mean + 1e-6) * in_gain_ref[...]).astype(BF16)

    @pl.when(holder)
    def _():
        pl.semaphore_wait(barrier, NZ - 1 + NP - 1 + NY - 1)

    @pl.when(jnp.logical_not(holder))
    def _():
        pl.semaphore_wait(barrier, NZ - 1)

    def id_copy(t, zt):
        return rcopy(id_src, idb.at[z], id_send.at[t], id_recv.at[z], at_z(zt))

    def v_copy(t, zt):
        return rcopy(vt.at[t], vbuf.at[z], v_send.at[t], v_recv.at[z], at_z(zt))

    for t in range(NT):
        zt = 3 * (t % 4) + t // 4

        @pl.when(z == zt)
        def _():
            idb[z] = id_src[...]

        @pl.when(z != zt)
        def _():
            id_copy(t, zt).start()

    for grp in range(2):
        wcopies[grp].wait()
        v = dot(normed, wv[grp]).astype(BF16)
        for t in range(4):
            vt[4 * grp + t] = v[:, LANES * t : LANES * (t + 1)]
        for k in range(4):
            q = lax.rem(zq + k, 4)
            t, zt = q + 4 * grp, 3 * q + grp

            @pl.when(z == zt)
            def _():
                vbuf[z] = vt[t]

            @pl.when(z != zt)
            def _():
                v_copy(t, zt).start()

    sub = lax.broadcasted_iota(jnp.int32, (ROWS, LANES), 0)
    lane = lax.broadcasted_iota(jnp.int32, (ROWS, LANES), 1)
    ones = jnp.ones((LANES, LANES), BF16)

    @pl.when(holder)
    def _():
        at = pl.ds(pl.multiple_of(tile * LANES, LANES), LANES)
        rate, log_keep = rate_ref[:, at], lk_ref[:, at]
        ones2 = jnp.ones((LANES, 2 * LANES), BF16)
        lane2 = lax.broadcasted_iota(jnp.int32, (ROWS, 2 * LANES), 1).astype(F32)
        usub = lax.broadcasted_iota(jnp.int32, (USERS, LANES), 0).astype(F32)

        for zz in range(NZ):
            @pl.when(z != zz)
            def _():
                rcopy(id_src, idb.at[zz], id_send.at[0], id_recv.at[zz], at_z(zz)).wait_recv()

        pre_q[0] = jnp.ones((USERS, LANES), F32)

        def prep(zz, carry):
            info = idb[zz]
            row, weight = info[0:1], 1.0 + 16.0 * info[1:2]
            col = dot(jnp.where(sub == lane, row, 0.0).astype(BF16), ones2)
            mt[zz] = (col == lane2).astype(F32).astype(BF16)
            after = jnp.where((col[:, :LANES] == row) & (lane > sub), weight, 0.0).astype(BF16)
            dcy[zz] = jnp.exp(decay_of(dot(after, ones), rate, log_keep))
            own = usub == row
            mem[zz] = own.astype(F32).astype(BF16)
            sp = jnp.exp(decay_of(dot(jnp.where(own, weight, 0.0).astype(BF16), ones), rate, log_keep))
            span[zz] = sp
            pre_q[zz + 1] = pre_q[zz] * sp
            return carry

        lax.fori_loop(0, NZ, prep, 0)

        def q1_copy(p):
            return rcopy(end_q.at[p], s1q.at[line], q1_send.at[p], q1_recv.at[line], at_line(p))

        def e1_copy(p):
            return rcopy(end_e.at[p], s1e.at[line], e1_send.at[p], e1_recv.at[line], at_line(p))

        def c_copy(p):
            return rcopy(cst.at[p], cbuf.at[line], c_send.at[p], c_recv.at[line], at_line(p))

        def yq_copy(yy):
            return rcopy(slab_q, yq.at[y], yq_send.at[yy], yq_recv.at[y], at_y(yy))

        def ye_copy(yy):
            return rcopy(slab_e, ye.at[y], ye_send.at[yy], ye_recv.at[y], at_y(yy))

        def to_parts(src, dst, value, copy):
            for p in range(NP):
                part = value[UP * p : UP * (p + 1)]

                @pl.when(line == p)
                def _():
                    dst[p] = part

                @pl.when(line != p)
                def _():
                    src[p] = part
                    copy(p).start()

        def from_parts(src, dst, ss, rs):
            for p in range(NP):
                @pl.when(line != p)
                def _():
                    rcopy(src.at[p], dst.at[p], ss.at[p], rs.at[p], at_line(p)).wait_recv()

        to_parts(end_q, s1q, pre_q[NZ], q1_copy)
        from_parts(end_q, s1q, q1_send, q1_recv)
        q = s1q[0]
        for p in range(1, NP):
            q = q * s1q[p]
        slab_q[...] = q
        for yy in range(1, NY):
            @pl.when(yy > y)
            def _():
                yq_copy(yy).start()

        def ends(zz, p):
            @pl.when(z != zz)
            def _():
                rcopy(vt.at[0], vbuf.at[zz], v_send.at[0], v_recv.at[zz], at_z(zz)).wait_recv()

            w = dcy[zz] * vbuf[zz].astype(F32)
            hi = w.astype(BF16)
            lo = (w - hi.astype(F32)).astype(BF16)
            member = mem[zz]
            e = dot(member, hi) + dot(member, lo)
            pre_p[zz] = p
            return span[zz] * p + e

        total = lax.fori_loop(0, NZ, ends, jnp.zeros((USERS, LANES), F32))

        to_parts(end_e, s1e, total, e1_copy)
        from_parts(end_e, s1e, e1_send, e1_recv)
        e = s1e[0]
        for p in range(1, NP):
            e = s1q[p] * e + s1e[p]
        slab_e[...] = e
        for yy in range(1, NY):
            @pl.when(yy > y)
            def _():
                ye_copy(yy).start()

        cacc[...] = jnp.zeros((UP, LANES), F32)
        for yy in range(NY - 1):
            @pl.when(yy < y)
            def _():
                rcopy(slab_q, yq.at[yy], yq_send.at[yy], yq_recv.at[yy], at_y(yy)).wait_recv()
                rcopy(slab_e, ye.at[yy], ye_send.at[yy], ye_recv.at[yy], at_y(yy)).wait_recv()
                cacc[...] = yq[yy] * cacc[...] + ye[yy]

        start = cacc[...]
        for p in range(NP):
            @pl.when(line == p)
            def _():
                cbuf[p] = start

            @pl.when(line != p)
            def _():
                cst[p] = start
                c_copy(p).start()

            start = s1q[p] * start + s1e[p]
        from_parts(cst, cbuf, c_send, c_recv)

        def r_copy(zz):
            return rcopy(rsrc.at[zz], rbuf.at[tile], r_send.at[zz], r_recv.at[tile], at_z(zz))

        carry_in = jnp.concatenate([cbuf[p] for p in range(NP)], axis=0)
        pad = jnp.zeros((2 * LANES - USERS, LANES), BF16)

        def give(k, carry):
            zz = lax.rem(z + k + 6, NZ)
            states = (pre_p[zz] + pre_q[zz] * carry_in).astype(BF16)
            rsrc[zz] = dot(mt[zz], jnp.concatenate([states, pad], axis=0)).astype(BF16)

            @pl.when(zz == z)
            def _():
                rbuf[tile] = rsrc[zz]

            @pl.when(zz != z)
            def _():
                r_copy(zz).start()

            return carry

        lax.fori_loop(0, NZ, give, 0)

        for p in range(NP):
            @pl.when(line != p)
            def _():
                q1_copy(p).wait_send()
                e1_copy(p).wait_send()
                c_copy(p).wait_send()
        for yy in range(1, NY):
            @pl.when(yy > y)
            def _():
                yq_copy(yy).wait_send()
                ye_copy(yy).wait_send()

    wcopies[2].wait()
    weight = 1.0 + 16.0 * brk
    col = dot(jnp.where(sub == lane, idr, 0.0).astype(BF16), ones)
    upto = (col == idr) & (lane <= sub)
    counts = dot(jnp.where(upto, weight, 0.0).astype(BF16), ones)
    within = upto.astype(F32).astype(BF16)
    breaks = jnp.floor(counts * (1.0 / 16.0))
    events_of = counts - 16.0 * breaks
    for t in range(NT):
        cols = slice(LANES * t, LANES * (t + 1))
        level = lk_ref[:, cols] * breaks - rate_ref[:, cols] * events_of
        grow[t] = jnp.exp(level)
        scaled = jnp.exp(-level) * vt[t].astype(F32)
        hi = scaled.astype(BF16)
        lo = (scaled - hi.astype(F32)).astype(BF16)
        xloc[t] = dot(within, hi) + dot(within, lo)
    gate = dot(normed, wg[...]).astype(BF16).astype(F32)
    gate = out_gain_ref[...] * (gate / (1.0 + jnp.exp(-gate)))
    for t in range(NT):
        sgate[t] = gate[:, LANES * t : LANES * (t + 1)]

    wcopies[3].wait()
    squares = jnp.zeros((ROWS, LANES), F32)
    for t in range(0, NT, 2):
        parts = []
        for u in (t, t + 1):
            zt = 3 * (u % 4) + u // 4

            @pl.when(z != zt)
            def _():
                rcopy(rsrc.at[0], rbuf.at[u], r_send.at[0], r_recv.at[u], at_z(zt)).wait_recv()

            h = grow[u] * (xloc[u] + rbuf[u].astype(F32))
            squares = squares + h * h
            parts.append((h * sgate[u]).astype(BF16))
        prod = dot(jnp.concatenate(parts, axis=1), wo[LANES * t : LANES * (t + 2), :])
        if t == 0:
            acc[...] = prod
        else:
            acc[...] += prod
    mean_h = jnp.sum(squares, axis=1, keepdims=True) * (1.0 / full)
    out_ref[...] = (ev_ref[...].astype(F32) + acc[...] * lax.rsqrt(mean_h + 1e-6)).astype(BF16)

    for t in range(NT):
        zt = 3 * (t % 4) + t // 4

        @pl.when(z != zt)
        def _():
            id_copy(t, zt).wait_send()
            v_copy(t, zt).wait_send()

    @pl.when(holder)
    def _():
        for zz in range(NZ):
            @pl.when(z != zz)
            def _():
                rcopy(rsrc.at[zz], rbuf.at[tile], r_send.at[zz], r_recv.at[tile], at_z(zz)).wait_send()


def on_device(NC, NX, NY, events, user_ids, session_break, in_gain, in_weight, decay_rates, keep_factor, out_gain, out_weight):
    NP = NC * NX
    UP = USERS // NP
    D = NT * LANES
    vmem = pl.BlockSpec(memory_space=pltpu.VMEM)
    hbm = pl.BlockSpec(memory_space=pl.ANY)
    V = pltpu.VMEM
    dma = lambda *n: pltpu.SemaphoreType.DMA(n)
    return pl.pallas_call(
        functools.partial(kernel, NC, NX, NY),
        out_shape=jax.ShapeDtypeStruct((ROWS, D), BF16),
        in_specs=[vmem] * 7 + [hbm] * 2,
        out_specs=vmem,
        scratch_shapes=[
            V((2, D, D // 2), BF16), V((D, D), BF16), V((D, D), BF16),
            V((NT, ROWS, LANES), BF16), V((8, LANES), F32), V((NZ, 8, LANES), F32),
            V((NZ, ROWS, LANES), BF16), V((NZ, ROWS, 2 * LANES), BF16), V((NZ, USERS, LANES), BF16),
            V((NZ, ROWS, LANES), F32), V((NZ, USERS, LANES), F32), V((NZ + 1, USERS, LANES), F32),
            V((NZ, USERS, LANES), F32),
            V((NP, UP, LANES), F32), V((NP, UP, LANES), F32), V((NP, UP, LANES), F32), V((NP, UP, LANES), F32),
            V((UP, LANES), F32), V((UP, LANES), F32), V((NY, UP, LANES), F32), V((NY, UP, LANES), F32),
            V((NP, UP, LANES), F32), V((NP, UP, LANES), F32), V((UP, LANES), F32),
            V((NZ, ROWS, LANES), BF16), V((NT, ROWS, LANES), BF16),
            V((NT, ROWS, LANES), F32), V((NT, ROWS, LANES), F32), V((NT, ROWS, LANES), F32),
            V((ROWS, D), F32), V((1, D), F32),
            dma(4), dma(NT), dma(NZ), dma(NT), dma(NZ), dma(NP), dma(NP), dma(NP), dma(NP),
            dma(NY), dma(NY), dma(NY), dma(NY), dma(NP), dma(NP), dma(NZ), dma(NT),
        ],
        compiler_params=pltpu.CompilerParams(
            collective_id=0, has_side_effects=True, vmem_limit_bytes=48 * 1024 * 1024
        ),
    )(
        events, user_ids.reshape(1, ROWS), session_break.reshape(1, ROWS),
        in_gain.reshape(1, D), decay_rates.reshape(1, D), keep_factor.reshape(1, D),
        out_gain.reshape(1, D), in_weight, out_weight,
    )


def solution(mesh):
    groups, shards = mesh.shape["grp"], mesh.shape["shard"]
    NC = 2 if groups % 2 == 0 else 1
    body = functools.partial(on_device, NC, shards // NZ, groups // NC)
    both = P(("grp", "shard"))
    return jax.shard_map(
        body,
        mesh=mesh,
        in_specs=(P(("grp", "shard"), None), both, both, P(), P(), P(), P(), P(), P()),
        out_specs=P(("grp", "shard"), None),
        check_vma=False,
    )
```

time: 323 us -> 72.4 us (0.22)
  the two profiles are of different devices: /device:TPU:6 before, /device:TPU:48 now
where the time goes in v1:
time: 72.4 us; the launch traced here: 72.1 us
  Pallas kernels  64.7 us (89%)
  local copies, waits for them, and re-layouts  7.3 us (10%)
    pallas_call x1, Pallas kernels, on_device(): pl.pallas_call(functools.partial(kernel, NC, NX, NY), out_shape=jax.Shape...  64.7 us
    unnamed x17, local copies, waits for them, and re-layouts  7.3 us

profile of v1, /device:TPU:48, one launch (start us, length us, event | category | flops | bytes accessed | tf_op | source)
XLA Modules:
  0.0 72.1 jit_solution(16448304811448807581)
XLA Ops:
  0.0 0.0 copy-start
  0.0 1.6 %copy-done = bf16[1024,1024]{1,0:T(8,128)(2,1)S(1)} copy-done((bf16[1024,1024]{1,0:T(8,128)(2,1)S(1)}, bf16[1024,1024]{1,0:T(8,128)(2,1)}, u32[]{:S(2)}) %copy-start) | copy-done | bytes 2097176
  1.6 0.0 copy-start.1
  1.6 0.9 %copy-done.1 = bf16[128,1024]{1,0:T(8,128)(2,1)S(1)} copy-done((bf16[128,1024]{1,0:T(8,128)(2,1)S(1)}, bf16[128,1024]{1,0:T(8,128)(2,1)}, u32[]{:S(2)}) %copy-start.1) | copy-done | bytes 262168
  2.5 0.0 copy-start.2
  2.5 0.7 copy-done.2
  3.2 0.0 copy-start.3
  3.2 0.7 copy-done.3
  3.9 0.0 copy-start.4
  3.9 0.7 copy-done.4
  4.6 0.0 copy-start.5
  4.6 0.7 copy-done.5
  5.3 0.0 copy-start.6
  5.3 0.7 copy-done.6
  5.9 0.0 copy-start.7
  6.0 0.7 copy-done.7
  6.6 64.7 %shard_map.91 = bf16[128,1024]{1,0:T(8,128)(2,1)S(1)} custom-call(bf16[128,1024]{1,0:T(8,128)(2,1)S(1)} %copy-done.1, s32[1,128]{1,0:T(1,128)S(1)} %bitcast.10, s32[1,128]{1,0:T(1,128)S(1)} %bitcast.11, f32[1,1024]{1,0:T(1,128)S(1)} %bitcast.6, f32[1,1024]{1,0:T(1,128)S(1)} %bitcast.7, f32[1,1024]{1,0:T(1,128)S(1)} %bitcast.8, f32[1,1024]{1,0:T(1,128)S(1)} %bitcast.9, ...), custom_call_target="tpu_custom_call" | custom-call | tf_op jit(solution)/shard_map/pallas_call | solution.py:365
  71.4 0.7 copy.11
Async XLA Ops:
  0.0 1.6 %copy-start = (bf16[1024,1024]{1,0:T(8,128)(2,1)S(1)}, bf16[1024,1024]{1,0:T(8,128)(2,1)}, u32[]{:S(2)}) copy-start(bf16[1024,1024]{1,0:T(8,128)(2,1)} %w_out.1) | copy-start | bytes 6291460
  1.6 0.9 %copy-start.1 = (bf16[128,1024]{1,0:T(8,128)(2,1)S(1)}, bf16[128,1024]{1,0:T(8,128)(2,1)}, u32[]{:S(2)}) copy-start(bf16[128,1024]{1,0:T(8,128)(2,1)} %ev_ref.1) | copy-start | bytes 786436
  2.5 0.7 copy-start.2
  3.2 0.7 copy-start.3
  3.9 0.7 copy-start.4
  4.6 0.7 copy-start.5
  5.3 0.7 copy-start.6
  5.9 0.7 copy-start.7

commit v2 on v1

v2 whole, which is shorter than its diff:
```python
import functools

import jax
import jax.numpy as jnp
from jax import lax
from jax.experimental import pallas as pl
from jax.experimental.pallas import tpu as pltpu
from jax.sharding import PartitionSpec as P

F32, BF16 = jnp.float32, jnp.bfloat16
MESH = pl.DeviceIdType.MESH
NZ = 12
NT = 8
LANES = 128
ROWS = 128
USERS = 192
GROUP = 4


def dot(a, b):
    return jnp.dot(a, b, preferred_element_type=F32)


def decay_of(counts, rate, log_keep):
    breaks = jnp.floor(counts * (1.0 / 16.0))
    return log_keep * breaks - rate * (counts - 16.0 * breaks)


def kernel(
    NC, NX, NY,
    ev_hbm, ids_hbm, brk_hbm, in_gain_hbm, rate_hbm, keep_hbm, out_gain_hbm, w_in, w_out,
    out_ref,
    ev_ref, ids_ref, brk_ref, in_gain_ref, rate_ref, keep_ref, out_gain_ref,
    wv, wg, wo, vt, id_src, idb, vbuf, mt, mem, dcy, span, pre_q, pre_p, end,
    end_e, end_q, s1e, s1q, slab_e, slab_q, ye, yq, cst, cbuf, cacc,
    rsrc, rbuf, xloc, grow, sgate, acc, lk_ref,
    op_sem, w_sem, id_send, id_recv, v_send, v_recv, q1_send, q1_recv, e1_send, e1_recv,
    yq_send, yq_recv, ye_send, ye_recv, c_send, c_recv, r_send, r_recv, ready,
):
    NP = NC * NX
    UP = USERS // NP
    g, s = lax.axis_index("grp"), lax.axis_index("shard")
    y, c = lax.div(g, NC), lax.rem(g, NC)
    x, z = lax.div(s, NZ), lax.rem(s, NZ)
    line = c * NX + x
    zq, zr = lax.div(z, 3), lax.rem(z, 3)
    holder = zr < 2
    tile = 2 * zq + zr

    def at_z(zz):
        return (g, x * NZ + zz)

    def at_line(p):
        return (y * NC + p // NX, (p % NX) * NZ + z)

    def at_y(yy):
        return (yy * NC + c, s)

    def rcopy(src, dst, ss, rs, dev):
        return pltpu.make_async_remote_copy(
            src_ref=src, dst_ref=dst, send_sem=ss, recv_sem=rs, device_id=dev, device_id_type=MESH
        )

    ocopies = [
        pltpu.make_async_copy(src, dst, op_sem.at[i])
        for i, (src, dst) in enumerate((
            (ids_hbm, ids_ref), (brk_hbm, brk_ref), (ev_hbm, ev_ref), (in_gain_hbm, in_gain_ref),
            (rate_hbm, rate_ref), (keep_hbm, keep_ref), (out_gain_hbm, out_gain_ref),
        ))
    ]
    for cp in ocopies:
        cp.start()
    half = NT * LANES // 2
    full = NT * LANES
    wcopies = [
        pltpu.make_async_copy(w_in.at[:, pl.ds(full, half)], wv.at[0], w_sem.at[0]),
        pltpu.make_async_copy(w_in.at[:, pl.ds(full + half, half)], wv.at[1], w_sem.at[1]),
        pltpu.make_async_copy(w_in.at[:, pl.ds(0, full)], wg, w_sem.at[2]),
        pltpu.make_async_copy(w_out, wo, w_sem.at[3]),
    ]
    for cp in wcopies[:2]:
        cp.start()

    barrier = pltpu.get_barrier_semaphore()
    for zz in range(1, NZ):
        @pl.when(z < zz)
        def _():
            pl.semaphore_signal(barrier, inc=1, device_id=at_z(zz), device_id_type=MESH)

    @pl.when(holder)
    def _():
        for d in range(1, NP):
            p = lax.rem(line + d, NP)
            pl.semaphore_signal(barrier, inc=1, device_id=(y * NC + lax.div(p, NX), lax.rem(p, NX) * NZ + z), device_id_type=MESH)
        for d in range(1, NY):
            pl.semaphore_signal(barrier, inc=1, device_id=at_y(lax.rem(y + d, NY)), device_id_type=MESH)

    for cp in ocopies[:2]:
        cp.wait()
    idr = ids_ref[...].astype(F32)
    brk = brk_ref[...].astype(F32)
    id_src[...] = jnp.concatenate([idr, brk, jnp.zeros((6, LANES), F32)], axis=0)

    @pl.when(holder)
    def _():
        pl.semaphore_wait(barrier, z + NP - 1 + NY - 1)

    @pl.when(jnp.logical_not(holder))
    def _():
        pl.semaphore_wait(barrier, z)

    for zz in range(NZ - 1):
        @pl.when((z > zz) & (holder if zz % 3 == 2 else z > zz))
        def _():
            pl.semaphore_signal(ready.at[z], inc=1, device_id=at_z(zz), device_id_type=MESH)

    def id_copy(t, zt):
        return rcopy(id_src, idb.at[z], id_send.at[t], id_recv.at[z], at_z(zt))

    def v_copy(t, zt):
        return rcopy(vt.at[t], vbuf.at[z], v_send.at[t], v_recv.at[z], at_z(zt))

    for t in range(NT):
        zt = 3 * (t // 2) + t % 2

        @pl.when(z == zt)
        def _():
            idb[z] = id_src[...]

        @pl.when(z > zt)
        def _():
            id_copy(t, zt).start()

    for cp in ocopies[2:]:
        cp.wait()
    lk_ref[...] = jnp.log(keep_ref[...])
    ev = ev_ref[...].astype(F32)
    mean = jnp.sum(ev * ev, axis=1, keepdims=True) * (1.0 / full)
    normed = (ev * lax.rsqrt(mean + 1e-6) * in_gain_ref[...]).astype(BF16)
    for grp in range(2):
        wcopies[grp].wait()
        if grp == 1:
            for cp in wcopies[2:]:
                cp.start()
        v = dot(normed, wv[grp]).astype(BF16)
        for t in range(4):
            vt[4 * grp + t] = v[:, LANES * t : LANES * (t + 1)]

    for t in range(NT):
        zt = 3 * (t // 2) + t % 2

        @pl.when(z < zt)
        def _():
            pl.semaphore_wait(ready.at[zt], 1)
            id_copy(t, zt).start()

        @pl.when(z == zt)
        def _():
            vbuf[z] = vt[t]

        @pl.when(z != zt)
        def _():
            v_copy(t, zt).start()

    sub = lax.broadcasted_iota(jnp.int32, (ROWS, LANES), 0)
    lane = lax.broadcasted_iota(jnp.int32, (ROWS, LANES), 1)
    ones = jnp.ones((LANES, LANES), BF16)

    wcopies[2].wait()
    weight = 1.0 + 16.0 * brk
    col = dot(jnp.where(sub == lane, idr, 0.0).astype(BF16), ones)
    upto = (col == idr) & (lane <= sub)
    counts = dot(jnp.where(upto, weight, 0.0).astype(BF16), ones)
    within = upto.astype(F32).astype(BF16)
    within = jnp.concatenate([within, within], axis=1)
    breaks = jnp.floor(counts * (1.0 / 16.0))
    events_of = counts - 16.0 * breaks
    for t in range(NT):
        cols = slice(LANES * t, LANES * (t + 1))
        level = lk_ref[:, cols] * breaks - rate_ref[:, cols] * events_of
        grow[t] = jnp.exp(level)
        scaled = jnp.exp(-level) * vt[t].astype(F32)
        hi = scaled.astype(BF16)
        lo = (scaled - hi.astype(F32)).astype(BF16)
        xloc[t] = dot(within, jnp.concatenate([hi, lo], axis=0))
    gate = dot(normed, wg[...]).astype(BF16).astype(F32)
    gate = out_gain_ref[...] * (gate / (1.0 + jnp.exp(-gate)))
    for t in range(NT):
        sgate[t] = gate[:, LANES * t : LANES * (t + 1)]

    @pl.when(holder)
    def _():
        at = pl.ds(pl.multiple_of(tile * LANES, LANES), LANES)
        rate, log_keep = rate_ref[:, at], lk_ref[:, at]
        ones2 = jnp.ones((LANES, 2 * LANES), BF16)
        lane2 = lax.broadcasted_iota(jnp.int32, (ROWS, 2 * LANES), 1).astype(F32)
        usub = lax.broadcasted_iota(jnp.int32, (USERS, LANES), 0).astype(F32)

        pre_q[0] = jnp.ones((USERS, LANES), F32)

        def prep(zz):
            info = idb[zz]
            row, weight = info[0:1], 1.0 + 16.0 * info[1:2]
            col = dot(jnp.where(sub == lane, row, 0.0).astype(BF16), ones2)
            mt[zz] = (col == lane2).astype(F32).astype(BF16)
            after = jnp.where((col[:, :LANES] == row) & (lane > sub), weight, 0.0).astype(BF16)
            dcy[zz] = jnp.exp(decay_of(dot(after, ones), rate, log_keep))
            own = usub == row
            own_b = own.astype(F32).astype(BF16)
            mem[zz] = jnp.concatenate([own_b, own_b], axis=1)
            sp = jnp.exp(decay_of(dot(jnp.where(own, weight, 0.0).astype(BF16), ones), rate, log_keep))
            span[zz] = sp
            pre_q[zz + 1] = pre_q[zz] * sp

        def prep_some(i, carry):
            for j in range(GROUP):
                zz = i * GROUP + j

                @pl.when(z != zz)
                def _():
                    rcopy(id_src, idb.at[zz], id_send.at[0], id_recv.at[zz], at_z(zz)).wait_recv()

            for j in range(GROUP):
                prep(i * GROUP + j)
            return carry

        lax.fori_loop(0, NZ // GROUP, prep_some, 0)

        def q1_copy(p):
            return rcopy(end_q.at[p], s1q.at[line], q1_send.at[p], q1_recv.at[line], at_line(p))

        def e1_copy(p):
            return rcopy(end_e.at[p], s1e.at[line], e1_send.at[p], e1_recv.at[line], at_line(p))

        def c_copy(p):
            return rcopy(cst.at[p], cbuf.at[line], c_send.at[p], c_recv.at[line], at_line(p))

        def yq_copy(yy):
            return rcopy(slab_q, yq.at[y], yq_send.at[yy], yq_recv.at[y], at_y(yy))

        def ye_copy(yy):
            return rcopy(slab_e, ye.at[y], ye_send.at[yy], ye_recv.at[y], at_y(yy))

        def to_parts(src, dst, value, copy):
            for p in range(NP):
                part = value[UP * p : UP * (p + 1)]

                @pl.when(line == p)
                def _():
                    dst[p] = part

                @pl.when(line != p)
                def _():
                    src[p] = part
                    copy(p).start()

        def from_parts(src, dst, ss, rs):
            for p in range(NP):
                @pl.when(line != p)
                def _():
                    rcopy(src.at[p], dst.at[p], ss.at[p], rs.at[p], at_line(p)).wait_recv()

        to_parts(end_q, s1q, pre_q[NZ], q1_copy)

        def spans_on():
            from_parts(end_q, s1q, q1_send, q1_recv)
            q = s1q[0]
            for p in range(1, NP):
                q = q * s1q[p]
            slab_q[...] = q
            for yy in range(1, NY):
                @pl.when(yy > y)
                def _():
                    yq_copy(yy).start()

        def ends(zz):
            w = dcy[zz] * vbuf[zz].astype(F32)
            hi = w.astype(BF16)
            lo = (w - hi.astype(F32)).astype(BF16)
            end[zz] = dot(mem[zz], jnp.concatenate([hi, lo], axis=0))

        total = jnp.zeros((USERS, LANES), F32)
        for i in range(0, NZ, GROUP):
            if i + GROUP == NZ:
                spans_on()
            for zz in range(i, i + GROUP):
                @pl.when(z != zz)
                def _():
                    rcopy(vt.at[0], vbuf.at[zz], v_send.at[0], v_recv.at[zz], at_z(zz)).wait_recv()

            for zz in range(i, i + GROUP):
                ends(zz)
            for zz in range(i, i + GROUP):
                pre_p[zz] = total
                total = span[zz] * total + end[zz]

        to_parts(end_e, s1e, total, e1_copy)
        from_parts(end_e, s1e, e1_send, e1_recv)
        e = s1e[0]
        for p in range(1, NP):
            e = s1q[p] * e + s1e[p]
        slab_e[...] = e
        for yy in range(1, NY):
            @pl.when(yy > y)
            def _():
                ye_copy(yy).start()

        cacc[...] = jnp.zeros((UP, LANES), F32)
        for yy in range(NY - 1):
            @pl.when(yy < y)
            def _():
                rcopy(slab_q, yq.at[yy], yq_send.at[yy], yq_recv.at[yy], at_y(yy)).wait_recv()
                rcopy(slab_e, ye.at[yy], ye_send.at[yy], ye_recv.at[yy], at_y(yy)).wait_recv()
                cacc[...] = yq[yy] * cacc[...] + ye[yy]

        start = cacc[...]
        for p in range(NP):
            @pl.when(line == p)
            def _():
                cbuf[p] = start

            @pl.when(line != p)
            def _():
                cst[p] = start
                c_copy(p).start()

            start = s1q[p] * start + s1e[p]
        from_parts(cst, cbuf, c_send, c_recv)

        def r_copy(zz):
            return rcopy(rsrc.at[zz], rbuf.at[tile], r_send.at[zz], r_recv.at[tile], at_z(zz))

        carry_in = jnp.concatenate([cbuf[p] for p in range(NP)], axis=0)
        pad = jnp.zeros((2 * LANES - USERS, LANES), BF16)

        def give(i, carry):
            blocks = [i * GROUP + j for j in range(GROUP)]
            for zz in blocks:
                states = (pre_p[zz] + pre_q[zz] * carry_in).astype(BF16)
                rsrc[zz] = dot(mt[zz], jnp.concatenate([states, pad], axis=0)).astype(BF16)
            for zz in blocks:
                @pl.when(zz == z)
                def _():
                    rbuf[tile] = rsrc[zz]

                @pl.when((zz > z) & (lax.rem(zz, 3) == 2))
                def _():
                    pl.semaphore_wait(ready.at[zz], 1)

                @pl.when(zz != z)
                def _():
                    r_copy(zz).start()

            return carry

        lax.fori_loop(0, NZ // GROUP, give, 0)

        for p in range(NP):
            @pl.when(line != p)
            def _():
                q1_copy(p).wait_send()
                e1_copy(p).wait_send()
                c_copy(p).wait_send()
        for yy in range(1, NY):
            @pl.when(yy > y)
            def _():
                yq_copy(yy).wait_send()
                ye_copy(yy).wait_send()

    wcopies[3].wait()
    squares = jnp.zeros((ROWS, LANES), F32)
    for t in range(0, NT, 2):
        parts = []
        for u in (t, t + 1):
            zt = 3 * (u // 2) + u % 2

            @pl.when(z != zt)
            def _():
                rcopy(rsrc.at[0], rbuf.at[u], r_send.at[0], r_recv.at[u], at_z(zt)).wait_recv()

            h = grow[u] * (xloc[u] + rbuf[u].astype(F32))
            squares = squares + h * h
            parts.append((h * sgate[u]).astype(BF16))
        prod = dot(jnp.concatenate(parts, axis=1), wo[LANES * t : LANES * (t + 2), :])
        if t == 0:
            acc[...] = prod
        else:
            acc[...] += prod
    mean_h = jnp.sum(squares, axis=1, keepdims=True) * (1.0 / full)
    out_ref[...] = (ev_ref[...].astype(F32) + acc[...] * lax.rsqrt(mean_h + 1e-6)).astype(BF16)

    for t in range(NT):
        zt = 3 * (t // 2) + t % 2

        @pl.when(z != zt)
        def _():
            id_copy(t, zt).wait_send()
            v_copy(t, zt).wait_send()

    @pl.when(holder)
    def _():
        for zz in range(NZ):
            @pl.when(z != zz)
            def _():
                rcopy(rsrc.at[zz], rbuf.at[tile], r_send.at[zz], r_recv.at[tile], at_z(zz)).wait_send()


def on_device(NC, NX, NY, events, user_ids, session_break, in_gain, in_weight, decay_rates, keep_factor, out_gain, out_weight):
    NP = NC * NX
    UP = USERS // NP
    D = NT * LANES
    vmem = pl.BlockSpec(memory_space=pltpu.VMEM)
    hbm = pl.BlockSpec(memory_space=pl.ANY)
    V = pltpu.VMEM
    dma = lambda *n: pltpu.SemaphoreType.DMA(n)
    return pl.pallas_call(
        functools.partial(kernel, NC, NX, NY),
        out_shape=jax.ShapeDtypeStruct((ROWS, D), BF16),
        in_specs=[hbm] * 9,
        out_specs=vmem,
        scratch_shapes=[
            V((ROWS, D), BF16), V((1, ROWS), jnp.int32), V((1, ROWS), jnp.int32),
            V((1, D), F32), V((1, D), F32), V((1, D), F32), V((1, D), F32),
            V((2, D, D // 2), BF16), V((D, D), BF16), V((D, D), BF16),
            V((NT, ROWS, LANES), BF16), V((8, LANES), F32), V((NZ, 8, LANES), F32),
            V((NZ, ROWS, LANES), BF16), V((NZ, ROWS, 2 * LANES), BF16), V((NZ, USERS, 2 * LANES), BF16),
            V((NZ, ROWS, LANES), F32), V((NZ, USERS, LANES), F32), V((NZ + 1, USERS, LANES), F32),
            V((NZ, USERS, LANES), F32), V((NZ, USERS, LANES), F32),
            V((NP, UP, LANES), F32), V((NP, UP, LANES), F32), V((NP, UP, LANES), F32), V((NP, UP, LANES), F32),
            V((UP, LANES), F32), V((UP, LANES), F32), V((NY, UP, LANES), F32), V((NY, UP, LANES), F32),
            V((NP, UP, LANES), F32), V((NP, UP, LANES), F32), V((UP, LANES), F32),
            V((NZ, ROWS, LANES), BF16), V((NT, ROWS, LANES), BF16),
            V((NT, ROWS, LANES), F32), V((NT, ROWS, LANES), F32), V((NT, ROWS, LANES), F32),
            V((ROWS, D), F32), V((1, D), F32),
            dma(7), dma(4), dma(NT), dma(NZ), dma(NT), dma(NZ), dma(NP), dma(NP), dma(NP), dma(NP),
            dma(NY), dma(NY), dma(NY), dma(NY), dma(NP), dma(NP), dma(NZ), dma(NT),
            pltpu.SemaphoreType.REGULAR((NZ,)),
        ],
        compiler_params=pltpu.CompilerParams(
            collective_id=0, has_side_effects=True, vmem_limit_bytes=60 * 1024 * 1024
        ),
    )(
        events, user_ids.reshape(1, ROWS), session_break.reshape(1, ROWS),
        in_gain.reshape(1, D), decay_rates.reshape(1, D), keep_factor.reshape(1, D),
        out_gain.reshape(1, D), in_weight, out_weight,
    )


def solution(mesh):
    groups, shards = mesh.shape["grp"], mesh.shape["shard"]
    NC = 2 if groups % 2 == 0 else 1
    body = functools.partial(on_device, NC, shards // NZ, groups // NC)
    both = P(("grp", "shard"))
    return jax.shard_map(
        body,
        mesh=mesh,
        in_specs=(P(("grp", "shard"), None), both, both, P(), P(), P(), P(), P(), P()),
        out_specs=P(("grp", "shard"), None),
        check_vma=False,
    )
```

time: 72.4 us -> 60.5 us (0.84)
  the two profiles are of different devices: /device:TPU:48 before, /device:TPU:185 now
where the time goes in v2:
time: 60.5 us; the launch traced here: 60.3 us
  Pallas kernels  58.6 us (97%)
  local copies, waits for them, and re-layouts  1.67 us (3%)
    pallas_call x1, Pallas kernels, on_device(): pl.pallas_call(functools.partial(kernel, NC, NX, NY), out_shape=jax.Shape...  58.6 us
    unnamed x1, local copies, waits for them, and re-layouts  1.67 us

profile of v2, /device:TPU:185, one launch (start us, length us, event | category | flops | bytes accessed | tf_op | source)
XLA Modules:
  0.0 60.3 jit_solution(9262547093938245243)
XLA Ops:
  0.0 58.6 %shard_map.91 = bf16[128,1024]{1,0:T(8,128)(2,1)} custom-call(bf16[128,1024]{1,0:T(8,128)(2,1)} %ev_hbm.1, s32[1,128]{1,0:T(1,128)} %bitcast.10, s32[1,128]{1,0:T(1,128)} %bitcast.11, f32[1,1024]{1,0:T(1,128)} %bitcast.6, f32[1,1024]{1,0:T(1,128)} %bitcast.7, f32[1,1024]{1,0:T(1,128)} %bitcast.8, f32[1,1024]{1,0:T(1,128)} %bitcast.9, ...), custom_call_target="tpu_custom_call" | custom-call | tf_op jit(solution)/shard_map/pallas_call | solution.py:416
  58.6 1.7 %copy.11 = bf16[128,1024]{1,0:T(8,128)(2,1)} copy(bf16[128,1024]{1,0:T(8,128)(2,1)} %shard_map.91) | data formatting | bytes 524288

commit v3 on v2

--- a/solution.py
+++ b/solution.py
@@ -35,7 +35,7 @@
     end_e, end_q, s1e, s1q, slab_e, slab_q, ye, yq, cst, cbuf, cacc,
     rsrc, rbuf, xloc, grow, sgate, acc, lk_ref,
     op_sem, w_sem, id_send, id_recv, v_send, v_recv, q1_send, q1_recv, e1_send, e1_recv,
-    yq_send, yq_recv, ye_send, ye_recv, c_send, c_recv, r_send, r_recv, ready,
+    yq_send, yq_recv, ye_send, ye_recv, c_send, c_recv, r_send, r_recv, ready, lines, go,
 ):
     NP = NC * NX
     UP = USERS // NP
@@ -43,9 +43,8 @@
     y, c = lax.div(g, NC), lax.rem(g, NC)
     x, z = lax.div(s, NZ), lax.rem(s, NZ)
     line = c * NX + x
-    zq, zr = lax.div(z, 3), lax.rem(z, 3)
-    holder = zr < 2
-    tile = 2 * zq + zr
+    holder = (lax.rem(z, 4) < 3) & (z < 10)
+    tile = z - lax.div(z, 4)
 
     def at_z(zz):
         return (g, x * NZ + zz)
@@ -87,13 +86,19 @@
         def _():
             pl.semaphore_signal(barrier, inc=1, device_id=at_z(zz), device_id_type=MESH)
 
-    @pl.when(holder)
-    def _():
+    def tell_peers(sem):
         for d in range(1, NP):
             p = lax.rem(line + d, NP)
-            pl.semaphore_signal(barrier, inc=1, device_id=(y * NC + lax.div(p, NX), lax.rem(p, NX) * NZ + z), device_id_type=MESH)
+            peer = (y * NC + lax.div(p, NX), lax.rem(p, NX) * NZ + z)
+            pl.semaphore_signal(sem, inc=1, device_id=peer, device_id_type=MESH)
         for d in range(1, NY):
-            pl.semaphore_signal(barrier, inc=1, device_id=at_y(lax.rem(y + d, NY)), device_id_type=MESH)
+            pl.semaphore_signal(sem, inc=1, device_id=at_y(lax.rem(y + d, NY)), device_id_type=MESH)
+
+    peers = NP - 1 + NY - 1
+
+    @pl.when(z == 0)
+    def _():
+        tell_peers(barrier)
 
     for cp in ocopies[:2]:
         cp.wait()
@@ -101,16 +106,16 @@
     brk = brk_ref[...].astype(F32)
     id_src[...] = jnp.concatenate([idr, brk, jnp.zeros((6, LANES), F32)], axis=0)
 
-    @pl.when(holder)
-    def _():
-        pl.semaphore_wait(barrier, z + NP - 1 + NY - 1)
-
-    @pl.when(jnp.logical_not(holder))
+    @pl.when(z == 0)
+    def _():
+        pl.semaphore_wait(barrier, peers)
+
+    @pl.when(z > 0)
     def _():
         pl.semaphore_wait(barrier, z)
 
     for zz in range(NZ - 1):
-        @pl.when((z > zz) & (holder if zz % 3 == 2 else z > zz))
+        @pl.when((z > zz) & (z > zz if zz % 4 < 3 and zz < 10 else holder))
         def _():
             pl.semaphore_signal(ready.at[z], inc=1, device_id=at_z(zz), device_id_type=MESH)
 
@@ -121,7 +126,7 @@
         return rcopy(vt.at[t], vbuf.at[z], v_send.at[t], v_recv.at[z], at_z(zt))
 
     for t in range(NT):
-        zt = 3 * (t // 2) + t % 2
+        zt = t + t // 3
 
         @pl.when(z == zt)
         def _():
@@ -147,7 +152,7 @@
             vt[4 * grp + t] = v[:, LANES * t : LANES * (t + 1)]
 
     for t in range(NT):
-        zt = 3 * (t // 2) + t % 2
+        zt = t + t // 3
 
         @pl.when(z < zt)
         def _():
@@ -161,6 +166,10 @@
         @pl.when(z != zt)
         def _():
             v_copy(t, zt).start()
+
+    @pl.when(z == 0)
+    def _():
+        tell_peers(lines)
 
     sub = lax.broadcasted_iota(jnp.int32, (ROWS, LANES), 0)
     lane = lax.broadcasted_iota(jnp.int32, (ROWS, LANES), 1)
@@ -188,6 +197,12 @@
     for t in range(NT):
         sgate[t] = gate[:, LANES * t : LANES * (t + 1)]
 
+    @pl.when(z == 0)
+    def _():
+        pl.semaphore_wait(lines, peers)
+        for t in range(1, NT):
+            pl.semaphore_signal(go, inc=1, device_id=at_z(t + t // 3), device_id_type=MESH)
+
     @pl.when(holder)
     def _():
         at = pl.ds(pl.multiple_of(tile * LANES, LANES), LANES)
@@ -260,8 +275,6 @@
                 def _():
                     rcopy(src.at[p], dst.at[p], ss.at[p], rs.at[p], at_line(p)).wait_recv()
 
-        to_parts(end_q, s1q, pre_q[NZ], q1_copy)
-
         def spans_on():
             from_parts(end_q, s1q, q1_send, q1_recv)
             q = s1q[0]
@@ -282,7 +295,11 @@
         total = jnp.zeros((USERS, LANES), F32)
         for i in range(0, NZ, GROUP):
             if i + GROUP == NZ:
-                spans_on()
+                @pl.when(z > 0)
+                def _():
+                    pl.semaphore_wait(go, 1)
+
+                to_parts(end_q, s1q, pre_q[NZ], q1_copy)
             for zz in range(i, i + GROUP):
                 @pl.when(z != zz)
                 def _():
@@ -295,6 +312,7 @@
                 total = span[zz] * total + end[zz]
 
         to_parts(end_e, s1e, total, e1_copy)
+        spans_on()
         from_parts(end_e, s1e, e1_send, e1_recv)
         e = s1e[0]
         for p in range(1, NP):
@@ -343,7 +361,7 @@
                 def _():
                     rbuf[tile] = rsrc[zz]
 
-                @pl.when((zz > z) & (lax.rem(zz, 3) == 2))
+                @pl.when((zz > z) & ((lax.rem(zz, 4) == 3) | (zz >= 10)))
                 def _():
                     pl.semaphore_wait(ready.at[zz], 1)
 
@@ -372,7 +390,7 @@
     for t in range(0, NT, 2):
         parts = []
         for u in (t, t + 1):
-            zt = 3 * (u // 2) + u % 2
+            zt = u + u // 3
 
             @pl.when(z != zt)
             def _():
@@ -390,7 +408,7 @@
     out_ref[...] = (ev_ref[...].astype(F32) + acc[...] * lax.rsqrt(mean_h + 1e-6)).astype(BF16)
 
     for t in range(NT):
-        zt = 3 * (t // 2) + t % 2
+        zt = t + t // 3
 
         @pl.when(z != zt)
         def _():
@@ -434,7 +452,7 @@
             V((ROWS, D), F32), V((1, D), F32),
             dma(7), dma(4), dma(NT), dma(NZ), dma(NT), dma(NZ), dma(NP), dma(NP), dma(NP), dma(NP),
             dma(NY), dma(NY), dma(NY), dma(NY), dma(NP), dma(NP), dma(NZ), dma(NT),
-            pltpu.SemaphoreType.REGULAR((NZ,)),
+            pltpu.SemaphoreType.REGULAR((NZ,)), pltpu.SemaphoreType.REGULAR, pltpu.SemaphoreType.REGULAR,
         ],
         compiler_params=pltpu.CompilerParams(
             collective_id=0, has_side_effects=True, vmem_limit_bytes=60 * 1024 * 1024

time: 60.5 us -> 57.2 us (0.945)
  the two profiles are of different devices: /device:TPU:185 before, /device:TPU:176 now
where the time goes in v3:
time: 57.2 us; the launch traced here: 57 us
  Pallas kernels  55.3 us (97%)
  local copies, waits for them, and re-layouts  1.67 us (3%)
    pallas_call x1, Pallas kernels, on_device(): pl.pallas_call(functools.partial(kernel, NC, NX, NY), out_shape=jax.Shape...  55.3 us
    unnamed x1, local copies, waits for them, and re-layouts  1.67 us

profile of v3, /device:TPU:176, one launch (start us, length us, event | category | flops | bytes accessed | tf_op | source)
XLA Modules:
  0.0 57.0 jit_solution(5052959746970771491)
XLA Ops:
  0.0 55.3 %shard_map.91 = bf16[128,1024]{1,0:T(8,128)(2,1)} custom-call(bf16[128,1024]{1,0:T(8,128)(2,1)} %ev_hbm.1, s32[1,128]{1,0:T(1,128)} %bitcast.10, s32[1,128]{1,0:T(1,128)} %bitcast.11, f32[1,1024]{1,0:T(1,128)} %bitcast.6, f32[1,1024]{1,0:T(1,128)} %bitcast.7, f32[1,1024]{1,0:T(1,128)} %bitcast.8, f32[1,1024]{1,0:T(1,128)} %bitcast.9, ...), custom_call_target="tpu_custom_call" | custom-call | tf_op jit(solution)/shard_map/pallas_call | solution.py:434
  55.3 1.7 %copy.11 = bf16[128,1024]{1,0:T(8,128)(2,1)} copy(bf16[128,1024]{1,0:T(8,128)(2,1)} %shard_map.91) | data formatting | bytes 524288

commit v4 on v3

--- a/solution.py
+++ b/solution.py
@@ -100,24 +100,24 @@
     def _():
         tell_peers(barrier)
 
+    @pl.when(z == 0)
+    def _():
+        pl.semaphore_wait(barrier, peers)
+
+    @pl.when(z > 0)
+    def _():
+        pl.semaphore_wait(barrier, z)
+
+    for zz in range(NZ - 1):
+        @pl.when((z > zz) & (z > zz if zz % 4 < 3 and zz < 10 else holder))
+        def _():
+            pl.semaphore_signal(ready.at[z], inc=1, device_id=at_z(zz), device_id_type=MESH)
+
     for cp in ocopies[:2]:
         cp.wait()
     idr = ids_ref[...].astype(F32)
     brk = brk_ref[...].astype(F32)
     id_src[...] = jnp.concatenate([idr, brk, jnp.zeros((6, LANES), F32)], axis=0)
-
-    @pl.when(z == 0)
-    def _():
-        pl.semaphore_wait(barrier, peers)
-
-    @pl.when(z > 0)
-    def _():
-        pl.semaphore_wait(barrier, z)
-
-    for zz in range(NZ - 1):
-        @pl.when((z > zz) & (z > zz if zz % 4 < 3 and zz < 10 else holder))
-        def _():
-            pl.semaphore_signal(ready.at[z], inc=1, device_id=at_z(zz), device_id_type=MESH)
 
     def id_copy(t, zt):
         return rcopy(id_src, idb.at[z], id_send.at[t], id_recv.at[z], at_z(zt))
@@ -148,24 +148,33 @@
             for cp in wcopies[2:]:
                 cp.start()
         v = dot(normed, wv[grp]).astype(BF16)
-        for t in range(4):
-            vt[4 * grp + t] = v[:, LANES * t : LANES * (t + 1)]
-
-    for t in range(NT):
-        zt = t + t // 3
-
-        @pl.when(z < zt)
-        def _():
-            pl.semaphore_wait(ready.at[zt], 1)
-            id_copy(t, zt).start()
-
-        @pl.when(z == zt)
-        def _():
-            vbuf[z] = vt[t]
-
-        @pl.when(z != zt)
-        def _():
-            v_copy(t, zt).start()
+        for k in range(4):
+            vt[4 * grp + k] = v[:, LANES * k : LANES * (k + 1)]
+
+    def send_values(order):
+        for t in order:
+            zt = t + t // 3
+
+            @pl.when(z < zt)
+            def _():
+                pl.semaphore_wait(ready.at[zt], 1)
+                id_copy(t, zt).start()
+
+            @pl.when(z == zt)
+            def _():
+                vbuf[z] = vt[t]
+
+            @pl.when(z != zt)
+            def _():
+                v_copy(t, zt).start()
+
+    @pl.when(z < 7)
+    def _():
+        send_values(range(NT))
+
+    @pl.when(z >= 7)
+    def _():
+        send_values((0, 5, 1, 4, 2, 3, 7, 6))
 
     @pl.when(z == 0)
     def _():
@@ -281,7 +290,7 @@
             for p in range(1, NP):
                 q = q * s1q[p]
             slab_q[...] = q
-            for yy in range(1, NY):
+            for yy in range(NY - 1, 0, -1):
                 @pl.when(yy > y)
                 def _():
                     yq_copy(yy).start()
@@ -318,7 +327,7 @@
         for p in range(1, NP):
             e = s1q[p] * e + s1e[p]
         slab_e[...] = e
-        for yy in range(1, NY):
+        for yy in range(NY - 1, 0, -1):
             @pl.when(yy > y)
             def _():
                 ye_copy(yy).start()
@@ -351,8 +360,7 @@
         carry_in = jnp.concatenate([cbuf[p] for p in range(NP)], axis=0)
         pad = jnp.zeros((2 * LANES - USERS, LANES), BF16)
 
-        def give(i, carry):
-            blocks = [i * GROUP + j for j in range(GROUP)]
+        def give(blocks):
             for zz in blocks:
                 states = (pre_p[zz] + pre_q[zz] * carry_in).astype(BF16)
                 rsrc[zz] = dot(mt[zz], jnp.concatenate([states, pad], axis=0)).astype(BF16)
@@ -361,17 +369,17 @@
                 def _():
                     rbuf[tile] = rsrc[zz]
 
-                @pl.when((zz > z) & ((lax.rem(zz, 4) == 3) | (zz >= 10)))
-                def _():
-                    pl.semaphore_wait(ready.at[zz], 1)
+                if zz % 4 == 3 or zz >= 10:
+                    @pl.when(zz > z)
+                    def _():
+                        pl.semaphore_wait(ready.at[zz], 1)
 
                 @pl.when(zz != z)
                 def _():
                     r_copy(zz).start()
 
-            return carry
-
-        lax.fori_loop(0, NZ // GROUP, give, 0)
+        for blocks in ((0,), (1, 2), (3, 4, 5), (6, 7, 8), (9, 10, 11)):
+            give(blocks)
 
         for p in range(NP):
             @pl.when(line != p)
@@ -405,7 +413,7 @@
         else:
             acc[...] += prod
     mean_h = jnp.sum(squares, axis=1, keepdims=True) * (1.0 / full)
-    out_ref[...] = (ev_ref[...].astype(F32) + acc[...] * lax.rsqrt(mean_h + 1e-6)).astype(BF16)
+    out_ref[...] = acc[...] * lax.rsqrt(mean_h + 1e-6)
 
     for t in range(NT):
         zt = t + t // 3
@@ -431,9 +439,9 @@
     hbm = pl.BlockSpec(memory_space=pl.ANY)
     V = pltpu.VMEM
     dma = lambda *n: pltpu.SemaphoreType.DMA(n)
-    return pl.pallas_call(
+    part = pl.pallas_call(
         functools.partial(kernel, NC, NX, NY),
-        out_shape=jax.ShapeDtypeStruct((ROWS, D), BF16),
+        out_shape=jax.ShapeDtypeStruct((ROWS, D), F32),
         in_specs=[hbm] * 9,
         out_specs=vmem,
         scratch_shapes=[
@@ -462,6 +470,7 @@
         in_gain.reshape(1, D), decay_rates.reshape(1, D), keep_factor.reshape(1, D),
         out_gain.reshape(1, D), in_weight, out_weight,
     )
+    return (events.astype(F32) + part).astype(BF16)
 
 
 def solution(mesh):

time: 57.2 us -> 56.9 us (level)
  the two profiles are of different devices: /device:TPU:176 before, /device:TPU:120 now
where the time goes in v4:
time: 56.9 us; the launch traced here: 56.7 us
  Pallas kernels  54.9 us (96%)
  other arithmetic  1.8 us (3%)
    pallas_call x1, Pallas kernels, on_device(): pl.pallas_call(functools.partial(kernel, NC, NX, NY), out_shape=jax.Shape...  54.9 us
    convert_element_type x1, other arithmetic, on_device(): return (events.astype(F32) + part).astype(BF16)  1.8 us

profile of v4, /device:TPU:120, one launch (start us, length us, event | category | flops | bytes accessed | tf_op | source)
XLA Modules:
  0.0 56.7 jit_solution(17797070136404757581)
XLA Ops:
  0.0 0.0 copy-start
  0.0 54.9 %shard_map.91 = f32[128,1024]{1,0:T(8,128)} custom-call(bf16[128,1024]{1,0:T(8,128)(2,1)} %ev_hbm.1, s32[1,128]{1,0:T(1,128)} %bitcast.10, s32[1,128]{1,0:T(1,128)} %bitcast.11, f32[1,1024]{1,0:T(1,128)} %bitcast.6, f32[1,1024]{1,0:T(1,128)} %bitcast.7, f32[1,1024]{1,0:T(1,128)} %bitcast.8, f32[1,1024]{1,0:T(1,128)} %bitcast.9, bf16[1024,2048]{1,0:T(8,128)(2,1)} %w_in.1, ...), custom_call_target="tpu_custom_call" | custom-call | tf_op jit(solution)/shard_map/pallas_call | solution.py:442
  54.9 0.0 copy-done
  54.9 1.8 %add_convert_fusion = bf16[128,1024]{1,0:T(8,128)(2,1)} fusion(f32[128,1024]{1,0:T(8,128)} %shard_map.91, bf16[128,1024]{1,0:T(8,128)(2,1)S(1)} %copy-done), kind=kLoop, calls=%fused_computation | loop fusion | flops 393216 | bytes 1048576 | tf_op jit(solution)/shard_map/convert_element_type | solution.py:473
Async XLA Ops:
  0.0 54.9 %copy-start = (bf16[128,1024]{1,0:T(8,128)(2,1)S(1)}, bf16[128,1024]{1,0:T(8,128)(2,1)}, u32[]{:S(2)}) copy-start(bf16[128,1024]{1,0:T(8,128)(2,1)} %ev_hbm.1) | copy-start | bytes 786436

commit v5 on v3

--- a/solution.py
+++ b/solution.py
@@ -281,7 +281,7 @@
             for p in range(1, NP):
                 q = q * s1q[p]
             slab_q[...] = q
-            for yy in range(1, NY):
+            for yy in range(NY - 1, 0, -1):
                 @pl.when(yy > y)
                 def _():
                     yq_copy(yy).start()
@@ -318,7 +318,7 @@
         for p in range(1, NP):
             e = s1q[p] * e + s1e[p]
         slab_e[...] = e
-        for yy in range(1, NY):
+        for yy in range(NY - 1, 0, -1):
             @pl.when(yy > y)
             def _():
                 ye_copy(yy).start()

time: 57.2 us -> 55.9 us (0.977)
  Pallas kernels: 55.3 us -> 54 us
    pallas_call x1, Pallas kernels: 55.3 us -> 54 us  [on_device(): pl.pallas_call(functools.partial(kernel, NC, NX, NY), out_shape=jax.Shape...]
where the time goes in v5:
time: 55.9 us; the launch traced here: 55.7 us
  Pallas kernels  54 us (97%)
  local copies, waits for them, and re-layouts  1.67 us (3%)
    pallas_call x1, Pallas kernels, on_device(): pl.pallas_call(functools.partial(kernel, NC, NX, NY), out_shape=jax.Shape...  54 us
    unnamed x1, local copies, waits for them, and re-layouts  1.67 us

profile of v5, /device:TPU:176, one launch (start us, length us, event | category | flops | bytes accessed | tf_op | source)
XLA Modules:
  0.0 55.7 jit_solution(4631587438156704001)
XLA Ops:
  0.0 54.0 %shard_map.91 = bf16[128,1024]{1,0:T(8,128)(2,1)} custom-call(bf16[128,1024]{1,0:T(8,128)(2,1)} %ev_hbm.1, s32[1,128]{1,0:T(1,128)} %bitcast.10, s32[1,128]{1,0:T(1,128)} %bitcast.11, f32[1,1024]{1,0:T(1,128)} %bitcast.6, f32[1,1024]{1,0:T(1,128)} %bitcast.7, f32[1,1024]{1,0:T(1,128)} %bitcast.8, f32[1,1024]{1,0:T(1,128)} %bitcast.9, ...), custom_call_target="tpu_custom_call" | custom-call | tf_op jit(solution)/shard_map/pallas_call | solution.py:434
  54.1 1.7 %copy.11 = bf16[128,1024]{1,0:T(8,128)(2,1)} copy(bf16[128,1024]{1,0:T(8,128)(2,1)} %shard_map.91) | data formatting | bytes 524288
